TPU v7x, 256 devices: a whole 4x4x8 slice. The times are simulated.
256 devices in a mesh: freq: 64 (over y, z, x_lo), rcv: 4 (over x_hi, core).
Axes of the slice: x: 4 (x_hi: 2, x_lo: 2; x = x_hi * 2 + x_lo), y: 4, z: 8, core: 2. Of those that a mesh axis runs over, the one named last changes fastest.
Arguments:
- traces: bfloat16 [128, 4096, 1024], P('freq', 'rcv'), may hold values from -0.75 to 0.75
- downgoing: bfloat16 [64, 2, 4096, 2048], P('freq', None, 'rcv'), may hold values from -4 to 4
Outputs:
- reflectivity: float32 [64, 2048, 2, 128], P('freq', 'rcv')
All inputs are finite; a program needn't handle non-finite values.
Results may differ from a plain program's by a relative error of at most 0.0032.
Values may be sent and summed in bfloat16 or wider, within the bound.
A program may use at most 64 MiB of HBM per device.

v0:
```python
import math

import jax
import jax.numpy as jnp
from jax import lax
from jax.sharding import PartitionSpec as P

ITERS = 2


epsilon = 1e-06


def spectrum_table(count_time, count_freq):
    times = jnp.arange(count_time, dtype=jnp.int32)
    bins = jnp.arange(count_freq, dtype=jnp.int32) + 1
    phase = (times[:, None] * bins[None, :] % count_time).astype(jnp.float32) * (
        2.0 * math.pi / count_time
    )
    return jnp.stack([jnp.cos(phase), -jnp.sin(phase)], axis=-1).reshape(count_time, 2 * count_freq)


def forward_product(columns, vec_piece):
    width = vec_piece.shape[0]
    shots = vec_piece.shape[2]
    receivers = columns.shape[1]
    prod = jnp.einsum(
        "cnv,vm->cnm",
        columns,
        vec_piece.reshape(width, 2 * shots),
        preferred_element_type=jnp.float32,
    ).reshape(2, receivers, 2, shots)
    return jnp.stack([prod[0, :, 0] - prod[1, :, 1], prod[0, :, 1] + prod[1, :, 0]], axis=1)


def adjoint_product(columns, left_rounded):
    width = columns.shape[2]
    receivers = columns.shape[1]
    shots = left_rounded.shape[2]
    prod = jnp.einsum(
        "cnv,nm->cvm",
        columns,
        left_rounded.reshape(receivers, 2 * shots),
        preferred_element_type=jnp.float32,
    ).reshape(2, width, 2, shots)
    return jnp.stack([prod[0, :, 0] + prod[1, :, 1], prod[0, :, 1] - prod[1, :, 0]], axis=1)


def per_device(traces, downgoing):
    shots_local, receivers_local, samples = traces.shape
    nfreq = downgoing.shape[0] * lax.axis_size("freq")
    table = spectrum_table(samples, nfreq)
    spectrum = jnp.dot(
        traces.astype(jnp.float32).reshape(shots_local * receivers_local, samples),
        table,
        precision=lax.Precision.HIGHEST,
    ).reshape(shots_local, receivers_local, nfreq, 2)
    spectrum = spectrum.transpose(2, 1, 3, 0)
    rhs_local = lax.all_to_all(spectrum, "freq", split_axis=0, concat_axis=3, tiled=True)[0]
    operator = downgoing[0]

    def left_norm(left_vec):
        return lax.psum(jnp.sum(left_vec * left_vec), ("freq", "rcv"))

    def apply_adjoint(left_vec):
        rounded = left_vec.astype(jnp.bfloat16)
        return lax.psum_scatter(
            adjoint_product(operator, rounded), "rcv", scatter_dimension=0, tiled=True
        )

    def right_norm(right_vec):
        return lax.psum(jnp.sum(right_vec * right_vec), ("freq", "rcv"))

    beta_now = jnp.sqrt(left_norm(rhs_local) + epsilon)
    left_vec = rhs_local / beta_now
    right_vec = apply_adjoint(left_vec)
    alpha_now = jnp.sqrt(right_norm(right_vec) + epsilon)
    right_vec = right_vec / alpha_now
    search = right_vec
    solution = jnp.zeros_like(right_vec)
    phi_bar = beta_now
    rho_bar = alpha_now
    for step in range(ITERS):
        apply_rounded = right_vec.astype(jnp.bfloat16)
        left_vec = (
            forward_product(operator, lax.all_gather(apply_rounded, "rcv", axis=0, tiled=True))
            - alpha_now * left_vec
        )
        beta_now = jnp.sqrt(left_norm(left_vec) + epsilon)
        left_vec = left_vec / beta_now
        right_vec = apply_adjoint(left_vec) - beta_now * right_vec
        alpha_now = jnp.sqrt(right_norm(right_vec) + epsilon)
        right_vec = right_vec / alpha_now
        rho_new = jnp.sqrt(rho_bar * rho_bar + beta_now * beta_now)
        cosine = rho_bar / rho_new
        sine_val = beta_now / rho_new
        theta_step = sine_val * alpha_now
        rho_bar = -cosine * alpha_now
        phi_step = cosine * phi_bar
        phi_bar = sine_val * phi_bar
        solution = solution + phi_step / rho_new * search
        search = right_vec - theta_step / rho_new * search
    return solution[None]


def solution(mesh):
    return jax.shard_map(
        per_device,
        mesh=mesh,
        in_specs=(P("freq", "rcv", None), P("freq", None, "rcv", None)),
        out_specs=P("freq", "rcv", None, None),
        check_vma=False,
    )
```

profile of v0, /device:TPU:1, one launch (start us, length us, event | category | flops | bytes accessed | tf_op | source)
XLA Modules:
  0.0 695.1 jit_solution(6912028163061404873)
XLA Ops:
  8.5 6.4 convolution_bitcast_fusion
  16.3 40.4 %all_to_all.4 = f32[64,1024,2,2]{1,2,3,0:T(2,128)S(1)} all-to-all(f32[64,1024,2,2]{1,2,3,0:T(2,128)S(1)} %bitcast.97), channel_id=1, replica_groups=mesh['freq'=64,'rcv'=4] {'freq'}, dimensions={0} | all-to-all | bytes 2097152 | tf_op jit(solution)/shard_map/all_to_all | solution.py:59
  58.5 75.4 %psum.35 = f32[]{:T(128)} all-reduce(f32[]{:T(128)} %multiply_reduce_fusion.1), channel_id=1, replica_groups=mesh['freq'=64,'rcv'=4] {'freq','rcv'}, use_global_device_ids=true, to_apply=%region_1.2 | all-reduce | flops 1 | bytes 8 | tf_op jit(solution)/shard_map/psum | solution.py:63
  136.9 5.7 fusion.6
  146.6 2.6 copy.88
  150.6 2.9 pad_maximum_fusion
  154.9 58.9 %all-reduce.5.cloned.1.call-done = f32[2048,2,128]{2,1,0:T(2,128)} async-done(((f32[2048,2,128]{2,1,0:T(2,128)}), f32[2048,2,128]{2,1,0:T(2,128)}) %all-reduce.5.cloned.1.call-update) | async-done | bytes 2097168
  216.0 76.1 %psum.36 = f32[]{:T(128)} all-reduce(f32[]{:T(128)} %get-tuple-element.7), channel_id=1, replica_groups=mesh['freq'=64,'rcv'=4] {'freq','rcv'}, use_global_device_ids=true, to_apply=%region_4.5 | all-reduce | flops 1 | bytes 8 | tf_op jit(solution)/shard_map/psum | solution.py:72
  294.1 20.3 %all-gather.3.cloned.1.call-done = bf16[2048,2,128]{2,1,0:T(2,128)(2,1)} async-done(((bf16[512,2,128]{2,1,0:T(2,128)(2,1)}), bf16[2048,2,128]{2,1,0:T(2,128)(2,1)}) %all-gather.3.cloned.1.call-update) | async-done | bytes 1048592 | tf_op jit(solution)/shard_map/all_gather | solution.py:86
  316.9 5.7 fusion.4
  326.4 76.1 %psum.37 = f32[]{:T(128)} all-reduce(f32[]{:T(128)} %get-tuple-element.5), channel_id=1, replica_groups=mesh['freq'=64,'rcv'=4] {'freq','rcv'}, use_global_device_ids=true, to_apply=%region_6.7 | all-reduce | flops 1 | bytes 8 | tf_op jit(solution)/shard_map/psum | solution.py:63
  404.6 5.7 fusion.2
  412.3 2.6 copy.97
  414.9 2.5 copy.98
  417.5 2.5 copy.95
  420.0 2.5 copy.96
  425.9 2.9 pad_maximum_fusion.1
  429.1 60.9 %all-reduce.7.cloned.1.call-done = f32[2048,2,128]{2,1,0:T(2,128)} async-done(((f32[2048,2,128]{2,1,0:T(2,128)}), f32[2048,2,128]{2,1,0:T(2,128)}) %all-reduce.7.cloned.1.call-update) | async-done | bytes 2097168
  491.9 76.1 %psum.38 = f32[]{:T(128)} all-reduce(f32[]{:T(128)} %multiply_reduce_fusion.2), channel_id=1, replica_groups=mesh['freq'=64,'rcv'=4] {'freq','rcv'}, use_global_device_ids=true, to_apply=%region_9.10 | all-reduce | flops 1 | bytes 8 | tf_op jit(solution)/shard_map/psum | solution.py:72
  570.0 20.4 %all-gather.5.cloned.1.call-done = bf16[2048,2,128]{2,1,0:T(2,128)(2,1)} async-done(((bf16[512,2,128]{2,1,0:T(2,128)(2,1)}), bf16[2048,2,128]{2,1,0:T(2,128)(2,1)}) %all-gather.5.cloned.1.call-update) | async-done | bytes 1048592 | tf_op jit(solution)/shard_map/all_gather | solution.py:86
  590.4 3.8 copy.85
  594.1 6.1 fusion
  606.3 4.0 fusion.11
  610.3 76.1 %psum.39 = f32[]{:T(128)} all-reduce(f32[]{:T(128)} %fusion.11), channel_id=1, replica_groups=mesh['freq'=64,'rcv'=4] {'freq','rcv'}, use_global_device_ids=true, to_apply=%region_11.12 | all-reduce | flops 1 | bytes 8 | tf_op jit(solution)/shard_map/psum | solution.py:63
  (51 shorter events, 40.4 us)
Async XLA Ops:
  6.5 207.2 %all-reduce.5.cloned.1.call-start = ((), (), s32[]{:S(2)}) async-start(), calls=%async_computation.3 | async-start | bytes 4194304
  149.3 4.3 copy-start.1
  153.6 160.8 %all-gather.3.cloned.1.call-start = ((), (), s32[]{:S(2)}) async-start(), calls=%async_computation.1 | async-start | bytes 1310720 | tf_op jit(solution)/shard_map/all_gather | solution.py:86
  293.8 196.2 %all-reduce.7.cloned.1.call-start = ((), (), s32[]{:S(2)}) async-start(), calls=%async_computation.4 | async-start | bytes 4194304
  322.6 1.8 copy-start
  428.8 161.6 %all-gather.5.cloned.1.call-start = ((), (), s32[]{:S(2)}) async-start(), calls=%async_computation.2 | async-start | bytes 1310720 | tf_op jit(solution)/shard_map/all_gather | solution.py:86
Sparse Core Ops, SparseCore 0:
  153.7 60.0 all-reduce.4
  293.9 20.4 all-gather.2
  428.9 61.0 all-reduce.6
  569.9 20.4 all-gather.4
where the time goes:
time: 696 us; the launch traced here: 695 us
  blocking collectives  420 us (60%)
  waiting for transfers between devices  161 us (23%)
  local copies, waits for them, and re-layouts  37.8 us (5%)
  matrix products  29.7 us (4%)
  other arithmetic  28.3 us (4%)
  between operations  17.8 us (3%)
    psum x3, blocking collectives, left_norm(): return lax.psum(jnp.sum(left_vec * left_vec), ('freq', 'rcv'))  228 us
    psum x2, blocking collectives, right_norm(): return lax.psum(jnp.sum(right_vec * right_vec), ('freq', 'rcv'))  152 us
    unnamed x6, waiting for transfers between devices  120 us
    all_gather x2, waiting for transfers between devices, per_device(): lax.all_gather(apply_rounded, 'rcv', axis=0, tiled=True)  40.7 us
    all_to_all x1, blocking collectives, per_device(): lax.all_to_all(spectrum, 'freq', split_axis=0, concat_axis=3, tiled=True)[0]  40.4 us
    unnamed x14, local copies, waits for them, and re-layouts  16.7 us
  transfers between devices with their start and end apart: 4, of which 4 were waited for; matrix products, arithmetic and copies ran while one was open for 0% of the time, Pallas kernels for 0%

commit v1 on v0

v1 whole, which is shorter than its diff:
```python
import functools
import math

import jax
import jax.numpy as jnp
import ml_dtypes
import numpy as np
from jax import lax
from jax.experimental import pallas as pl
from jax.experimental.pallas import tpu as pltpu
from jax.sharding import PartitionSpec as P

EPS = 1e-06
MESH = pl.DeviceIdType.MESH
BF16 = jnp.bfloat16
F32 = jnp.float32
FREQS = 64
RCV = 4
SAMPLES = 1024
ROWS = 1024
COLS = 2048
BLK = 512
M = 128
SIGMA = 2.0**-10
TAU = 2.0**-8


def dft_table():
    times = np.arange(SAMPLES, dtype=np.int64)
    bins = np.arange(FREQS, dtype=np.int64) + 1
    phase = (bins[:, None] * times[None, :] % SAMPLES).astype(np.float64) * (2.0 * math.pi / SAMPLES)
    table = np.concatenate([np.cos(phase), -np.sin(phase)], axis=0) * SIGMA
    high = table.astype(ml_dtypes.bfloat16)
    low = (table - high.astype(np.float64)).astype(ml_dtypes.bfloat16)
    return np.concatenate([high, low], axis=0)


def lane_sums(x):
    acc = x[:, 0:128]
    for t in range(1, x.shape[1] // 128):
        acc = acc + x[:, t * 128 : (t + 1) * 128]
    return jnp.sum(acc, axis=0, keepdims=True)


def nt_dot(a, b):
    return lax.dot_general(a, b, (((1,), (1,)), ((), ())), preferred_element_type=F32)


def kernel(
    table_ref, traces_ref, oper_ref, out_ref,
    tr, op, s32, f32s, sb, rb, xu, xy, ps, pr, cc, cs, cr, cl, clr, vop, vn, yy, zz, tmp,
    ar_src, ar1, ar_mid, ar2,
    tr_sem, op_sem, a_ss, a_rs, p_ss, p_rs, x_ss, x_rs, g_ss, g_rs, l_ss, l_rs, r_ss, r_rs,
):
    f = lax.axis_index("freq")
    r = lax.axis_index("rcv")
    h = r // 2
    e = lax.rem(r, 2)
    sib = (f, h * 2 + 1 - e)
    xp = (f, (1 - h) * 2 + e)
    g1 = lax.rem(f, 16)
    fy = f // 16
    g2 = fy * 4 + r

    def peer1(d):
        return (fy * 16 + lax.rem(g1 + d, 16), r)

    def peer2(d):
        q = lax.rem(g2 + d, 16)
        return ((q // 4) * 16 + g1, lax.rem(q, 4))

    def local(src, dst, sem):
        return pltpu.make_async_copy(src, dst, sem)

    def remote(src, dst, ss, rs, to):
        return pltpu.make_async_remote_copy(
            src_ref=src, dst_ref=dst, send_sem=ss, recv_sem=rs, device_id=to, device_id_type=MESH
        )

    tr_copies = [local(traces_ref.at[s], tr.at[s], tr_sem.at[s]) for s in range(2)]
    for c in tr_copies:
        c.start()
    op_copy = local(oper_ref, op, op_sem)
    op_copy.start()

    barrier = pltpu.get_barrier_semaphore()

    def greet(d, c):
        pl.semaphore_signal(
            barrier, inc=1, device_id=(lax.rem(f + d, FREQS), r), device_id_type=MESH
        )
        return c

    lax.fori_loop(1, FREQS, greet, 0)

    def greet2(d, c):
        to = (lax.rem(fy + d // 3, 4) * 16 + g1, lax.rem(r + 1 + lax.rem(d, 3), 4))
        pl.semaphore_signal(barrier, inc=1, device_id=to, device_id_type=MESH)
        return c

    lax.fori_loop(0, 12, greet2, 0)

    def dft(s):
        tr_copies[s].wait()
        for q in range(4):
            res = nt_dot(table_ref[...], tr[s, q * 256 : (q + 1) * 256, :])
            d = res[0:128] + res[128:256]
            for c in range(2):
                for qq in range(2):
                    s32[pl.ds((q * 2 + qq) * 2 + c, FREQS, stride=16), :] = d[
                        c * 64 : (c + 1) * 64, qq * 128 : (qq + 1) * 128
                    ]
        sb[s] = s32[...].astype(BF16).reshape(FREQS, 16, 128)

    def a2a_send(s):
        def go(d, c):
            to = lax.rem(f + d, FREQS)
            remote(sb.at[s, to], rb.at[s, f], a_ss.at[s], a_rs.at[s], (to, r)).start()
            return c

        lax.fori_loop(1, FREQS, go, 0)
        rb[s, f] = sb[s, f]

    def a2a_wait(ref, sem, s):
        part = ref.at[s, pl.ds(0, FREQS - 1)]
        local(part, part, sem.at[s]).wait()

    def relayout(s):
        f32s[...] = rb[s].astype(F32).reshape(FREQS * 16, 128)
        total = jnp.zeros((FREQS, 128), F32)
        for q in range(8):
            lo, hi = q * 128, (q + 1) * 128
            re = f32s[pl.ds(q * 2, FREQS, stride=16), :]
            im = f32s[pl.ds(q * 2 + 1, FREQS, stride=16), :]
            total = total + re * re + im * im
            reb, imb = re.astype(BF16), im.astype(BF16)
            xu[s, 0:64, lo:hi] = reb
            xu[s, 64:128, lo:hi] = imb
            xu[s, 0:64, ROWS + lo : ROWS + hi] = imb
            xu[s, 64:128, ROWS + lo : ROWS + hi] = -reb
        return jnp.sum(total, axis=0, keepdims=True)

    def cols(b):
        return pl.ds(pl.multiple_of(b * BLK, BLK), BLK)

    def sib_copy(k, s, i):
        return remote(ps.at[k, s, i], pr.at[k, s, i], p_ss.at[k, s, i], p_rs.at[k, s, i], sib)

    def x_copy(k, s, i):
        return remote(cs.at[k, s, i], cr.at[k, s, i], x_ss.at[k, s, i], x_rs.at[k, s, i], xp)

    def ag_copy(k, s, i, b):
        part = vop.at[k, s, :, cols(b)]
        return remote(part, part, g_ss.at[k, s, i], g_rs.at[k, s, i], sib)

    def lo_copy(s):
        return remote(cl.at[s, 1 - h], clr.at[s], l_ss.at[s], l_rs.at[s], xp)

    def adjoint(k, x, s):
        for i in range(2):
            ps[k, s, i] = jnp.dot(x[s], op[:, cols(2 * i + 1 - e)], preferred_element_type=F32)
            sib_copy(k, s, i).start()
        for i in range(2):
            p = jnp.dot(x[s], op[:, cols(2 * i + e)], preferred_element_type=F32)
            sib_copy(k, s, i).wait_recv()
            c = p + pr[k, s, i]
            cb = c.astype(BF16)
            cc[k, s, i] = c
            cs[k, s, i] = cb
            if k == 0:
                cl[s, i] = (c - cb.astype(F32)).astype(BF16)
            x_copy(k, s, i).start()

    def gather(k, s):
        for i in range(2):
            x_copy(k, s, i).wait_recv()
            v = cc[k, s, i] + cr[k, s, i].astype(F32)
            cc[k, s, i] = v
            vop[k, s, :, cols(2 * i + e)] = v.astype(BF16)
            ag_copy(k, s, i, 2 * i + e).start()
        for i in range(2):
            ag_copy(k, s, i, 2 * i + 1 - e).wait_recv()

    def forward(k, s, dst):
        vn[0:64] = -vop[k, s, 64:128]
        vn[64:128] = vop[k, s, 0:64]
        for n in range(2):
            lo, hi = n * 512, (n + 1) * 512
            dst[s, :, lo:hi] = nt_dot(vop[k, s], op[lo:hi, :]) + nt_dot(vn[...], op[ROWS + lo : ROWS + hi, :])

    def operand(s):
        y = (yy[s] * TAU).astype(BF16)
        xy[s, :, 0:ROWS] = y
        xy[s, 0:64, ROWS:] = y[64:128]
        xy[s, 64:128, ROWS:] = -y[0:64]

    def ar_start(n, tile):
        ar_src[n] = tile
        ar1[n, 0] = tile

        def go(d, c):
            remote(ar_src.at[n], ar1.at[n, d], r_ss.at[n, 0], r_rs.at[n, 0], peer1(d)).start()
            return c

        lax.fori_loop(1, 16, go, 0)

    def ar_wait(ref, n, sem):
        part = ref.at[n, pl.ds(1, 15)]
        local(part, part, sem).wait()

    def ar_middle(n):
        ar_wait(ar1, n, r_rs.at[n, 0])
        tile = jnp.sum(ar1[n], axis=0)
        ar_mid[n] = tile
        ar2[n, 0] = tile

        def go(d, c):
            remote(ar_mid.at[n], ar2.at[n, d], r_ss.at[n, 1], r_rs.at[n, 1], peer2(d)).start()
            return c

        lax.fori_loop(1, 16, go, 0)

    def ar_end(n):
        ar_wait(ar2, n, r_rs.at[n, 1])
        return jnp.sum(jnp.sum(ar2[n], axis=0), axis=1, keepdims=True)

    def tile_of(row0, row1=None):
        at = lax.broadcasted_iota(jnp.int32, (8, 128), 0)
        tile = jnp.where(at == 0, row0, 0.0)
        if row1 is not None:
            tile = jnp.where(at == 1, row1, tile)
        return tile

    dft(0)
    pl.semaphore_wait(barrier, FREQS - 1 + 12)
    a2a_send(0)
    dft(1)
    a2a_send(1)
    op_copy.wait()

    sum_u = jnp.zeros((1, 128), F32)
    for s in range(2):
        a2a_wait(rb, a_rs, s)
        sum_u = sum_u + relayout(s)
        adjoint(0, xu, s)

    sum_v = jnp.zeros((1, 128), F32)
    for s in range(2):
        gather(0, s)
        v = cc[0, s, h]
        sum_v = sum_v + lane_sums(v * v)
        if s == 1:
            ar_start(0, tile_of(sum_u, sum_v))
        forward(0, s, yy)
        operand(s)
        if s == 1:
            ar_middle(0)
        adjoint(1, xy, s)
    total = ar_end(0)
    beta0_sq = total[0:1] * (1.0 / SIGMA**2) + EPS
    beta0 = jnp.sqrt(beta0_sq)
    sb0 = beta0 * SIGMA
    alpha0_sq = total[1:2] / (sb0 * sb0) + EPS
    alpha0 = jnp.sqrt(alpha0_sq)
    g0 = sb0 * alpha0
    row = jnp.zeros((1, 128), F32)
    for s in range(2):
        left = yy[s] - alpha0_sq * xu[s, :, 0:ROWS].astype(F32)
        row = row + lane_sums(left * left)
    ar_start(1, tile_of(row))

    gather(1, 0)
    ar_middle(1)
    forward(1, 0, zz)
    total = ar_end(1)
    beta1_sq = total[0:1] / (g0 * g0) + EPS
    beta1 = jnp.sqrt(beta1_sq)
    k1 = (alpha0_sq + beta1_sq) * TAU
    gather(1, 1)
    row = jnp.zeros((1, 128), F32)
    for s in range(2):
        right = cc[1, s, h] - k1 * cc[0, s, h]
        row = row + lane_sums(right * right)
    ar_start(2, tile_of(row))
    for s in range(2):
        lo_copy(s).start()
    forward(1, 1, zz)
    ar_middle(2)
    total = ar_end(2)
    g1s = g0 * beta1 * TAU
    alpha1_sq = total[0:1] / (g1s * g1s) + EPS
    alpha1 = jnp.sqrt(alpha1_sq)
    row = jnp.zeros((1, 128), F32)
    ky = k1 + alpha1_sq * TAU
    ku = alpha1_sq * alpha0_sq * TAU
    for s in range(2):
        left = zz[s] - ky * yy[s] + ku * xu[s, :, 0:ROWS].astype(F32)
        row = row + lane_sums(left * left)
    ar_start(3, tile_of(row))
    for s in range(2):
        lo_copy(s).wait_recv()
    ar_middle(3)
    total = ar_end(3)
    g2s = g1s * alpha1
    beta2_sq = total[0:1] / (g2s * g2s) + EPS

    rho1_sq = alpha0_sq + beta1_sq
    rho1 = jnp.sqrt(rho1_sq)
    cos1 = alpha0 / rho1
    sin1 = beta1 / rho1
    theta1 = sin1 * alpha1
    rhobar = cos1 * alpha1
    phi1 = cos1 * beta0
    phibar = sin1 * beta0
    rho2 = jnp.sqrt(rhobar * rhobar + beta2_sq)
    phi2 = (rhobar / rho2) * phibar
    y2 = -(phi2 / rho2)
    c_v = (phi1 / rho1 - y2 * (theta1 / rho1)) / g0
    c_r = y2 / g2s
    for s in range(2):
        v = cc[0, s, h] + clr[s].astype(F32)
        right = cc[1, s, h] - k1 * v
        x = c_v * v + c_r * right
        for c in range(2):
            for t in range(4):
                tmp[t, pl.ds(c * 128 + s, 64, stride=2), :] = x[
                    c * 64 : (c + 1) * 64, t * 128 : (t + 1) * 128
                ]
    for c in range(2):
        for t in range(4):
            out_ref[pl.ds(t * 256 + c, 128, stride=2), :] = tmp[t, c * 128 : (c + 1) * 128, :].T

    for s in range(2):
        a2a_wait(sb, a_ss, s)
        lo_copy(s).wait_send()
        for k in range(2):
            for i in range(2):
                sib_copy(k, s, i).wait_send()
                x_copy(k, s, i).wait_send()
                ag_copy(k, s, i, 2 * i + e).wait_send()
    for n in range(4):
        ar_wait(ar1, n, r_ss.at[n, 0])
        ar_wait(ar2, n, r_ss.at[n, 1])


def per_device(table, traces, downgoing):
    vmem = pltpu.VMEM
    dma = pltpu.SemaphoreType.DMA
    scratch = [
        vmem((2, ROWS, SAMPLES), BF16),
        vmem((2 * ROWS, COLS), BF16),
        vmem((FREQS * 16, 128), F32),
        vmem((FREQS * 16, 128), F32),
        vmem((2, FREQS, 16, 128), BF16),
        vmem((2, FREQS, 16, 128), BF16),
        vmem((2, M, 2 * ROWS), BF16),
        vmem((2, M, 2 * ROWS), BF16),
        vmem((2, 2, 2, M, BLK), F32),
        vmem((2, 2, 2, M, BLK), F32),
        vmem((2, 2, 2, M, BLK), F32),
        vmem((2, 2, 2, M, BLK), BF16),
        vmem((2, 2, 2, M, BLK), BF16),
        vmem((2, 2, M, BLK), BF16),
        vmem((2, M, BLK), BF16),
        vmem((2, 2, M, COLS), BF16),
        vmem((M, COLS), BF16),
        vmem((2, M, ROWS), F32),
        vmem((2, M, ROWS), F32),
        vmem((4, 2 * M, 128), F32),
        vmem((4, 8, 128), F32),
        vmem((4, 16, 8, 128), F32),
        vmem((4, 8, 128), F32),
        vmem((4, 16, 8, 128), F32),
        dma((2,)), dma,
        dma((2,)), dma((2,)),
        dma((2, 2, 2)), dma((2, 2, 2)),
        dma((2, 2, 2)), dma((2, 2, 2)),
        dma((2, 2, 2)), dma((2, 2, 2)),
        dma((2,)), dma((2,)),
        dma((4, 2)), dma((4, 2)),
    ]
    out = pl.pallas_call(
        kernel,
        out_shape=jax.ShapeDtypeStruct((2 * BLK, 128), F32),
        in_specs=[
            pl.BlockSpec(memory_space=pltpu.VMEM),
            pl.BlockSpec(memory_space=pl.ANY),
            pl.BlockSpec(memory_space=pl.ANY),
        ],
        out_specs=pl.BlockSpec(memory_space=pltpu.VMEM),
        scratch_shapes=scratch,
        compiler_params=pltpu.CompilerParams(
            collective_id=0, has_side_effects=True, vmem_limit_bytes=52 * 2**20
        ),
        name="lsqr",
    )(table, traces, downgoing.reshape(2 * ROWS, COLS))
    return out.reshape(1, BLK, 2, 128)


def solution(mesh):
    table = dft_table()
    return jax.shard_map(
        lambda traces, downgoing: per_device(jnp.asarray(table), traces, downgoing),
        mesh=mesh,
        in_specs=(P("freq", "rcv", None), P("freq", None, "rcv", None)),
        out_specs=P("freq", "rcv", None, None),
        check_vma=False,
    )
```

time: 696 us -> 91.2 us (0.13)
  blocking collectives: 420 us -> 0 us
  waiting for transfers between devices: 161 us -> 0 us
  Pallas kernels: 0 us -> 89.2 us
  local copies, waits for them, and re-layouts: 37.8 us -> 1.84 us
  matrix products: 29.7 us -> 0 us
  other arithmetic: 28.3 us -> 0 us
  between operations: 17.8 us -> 0.01 us
    psum x5 -> x0, blocking collectives: 380 us -> none  [the longest x3 228 us: left_norm(): return lax.psum(jnp.sum(left_vec * left_vec), ('freq', 'rcv'))]
    unnamed x6 -> x0, waiting for transfers between devices: 120 us -> none
    pallas_call x0 -> x1, Pallas kernels: none -> 89.2 us  [per_device(): pl.pallas_call(kernel, out_shape=jax.ShapeDtypeStruct((2 * BLK, 128), F32...]
    all_gather x2 -> x0, waiting for transfers between devices: 40.7 us -> none  [per_device(): lax.all_gather(apply_rounded, 'rcv', axis=0, tiled=True)]
    all_to_all x1 -> x0, blocking collectives: 40.4 us -> none  [per_device(): lax.all_to_all(spectrum, 'freq', split_axis=0, concat_axis=3, tiled=True)[0]]
    dot_general x5 -> x0, matrix products: 29.7 us -> none  [the longest x2 11.8 us: forward_product(): jnp.einsum('cnv,vm->cnm', columns, vec_piece.reshape(width, 2 * shots), p...]
    unnamed x14 -> x3, local copies, waits for them, and re-layouts: 16.7 us -> 1.84 us
    reduce_sum x5 -> x0, other arithmetic: 10.5 us -> none  [the longest x3 7.61 us: left_norm(): return lax.psum(jnp.sum(left_vec * left_vec), ('freq', 'rcv'))]
  transfers between devices with their start and end apart: 4 -> 0, of which waited for: 4 -> 0; matrix products, arithmetic and copies ran while one was open for 0% -> 0% of each run, Pallas kernels for 0% -> 0%
where the time goes in v1:
time: 91.2 us; the launch traced here: 91.1 us
  Pallas kernels  89.2 us (98%)
  local copies, waits for them, and re-layouts  1.84 us (2%)
    pallas_call x1, Pallas kernels, per_device(): pl.pallas_call(kernel, out_shape=jax.ShapeDtypeStruct((2 * BLK, 128), F32...  89.2 us
    unnamed x3, local copies, waits for them, and re-layouts  1.84 us

profile of v1, /device:TPU:1, one launch (start us, length us, event | category | flops | bytes accessed | tf_op | source)
XLA Modules:
  0.0 91.1 jit_solution(3296803537683125400)
XLA Ops:
  0.0 0.0 copy-start
  0.0 1.0 %copy-done = bf16[256,1024]{1,0:T(8,128)(2,1)S(1)} copy-done((bf16[256,1024]{1,0:T(8,128)(2,1)S(1)}, bf16[256,1024]{1,0:T(8,128)(2,1)}, u32[]{:S(2)}) %copy-start) | copy-done | bytes 524312
  1.0 89.2 %lsqr.1 = f32[1024,128]{1,0:T(8,128)S(1)} custom-call(bf16[256,1024]{1,0:T(8,128)(2,1)S(1)} %copy-done, bf16[2,1024,1024]{2,1,0:T(8,128)(2,1)} %traces_ref.1, bf16[2048,2048]{1,0:T(8,128)(2,1)} %bitcast.3), custom_call_target="tpu_custom_call" | custom-call | tf_op jit(solution)/shard_map/lsqr/pallas_call | solution.py:382
  90.3 0.8 copy.5
Async XLA Ops:
  0.0 1.0 %copy-start = (bf16[256,1024]{1,0:T(8,128)(2,1)S(1)}, bf16[256,1024]{1,0:T(8,128)(2,1)}, u32[]{:S(2)}) copy-start(bf16[256,1024]{1,0:T(8,128)(2,1)} %constant.2.clone.table_ref) | copy-start | bytes 1572868

commit v2 on v1

v2 whole, which is shorter than its diff:
```python
import math

import jax
import jax.numpy as jnp
import ml_dtypes
import numpy as np
from jax import lax
from jax.experimental import pallas as pl
from jax.experimental.pallas import tpu as pltpu
from jax.sharding import PartitionSpec as P

EPS = 1e-06
MESH = pl.DeviceIdType.MESH
BF16 = jnp.bfloat16
F32 = jnp.float32
FREQS = 64
RCV = 4
SAMPLES = 1024
ROWS = 1024
COLS = 2048
BLK = 512
M = 128
SIGMA = 2.0**-10
FAR_FIRST = (4, 3, 5, 2, 6, 1, 7, 0)
AR_NEAR = (8, 9, 7, 6, 10, 5, 11, 4, 12, 3, 13, 2, 14, 1, 15)
AR_FAR = (10, 9, 11, 8, 6, 14, 5, 7, 13, 15, 2, 4, 12, 1, 3)
TAU = 2.0**-8


def dft_table():
    times = np.arange(SAMPLES, dtype=np.int64)
    bins = np.arange(FREQS, dtype=np.int64) + 1
    phase = (bins[:, None] * times[None, :] % SAMPLES).astype(np.float64) * (2.0 * math.pi / SAMPLES)
    table = np.concatenate([np.cos(phase), -np.sin(phase)], axis=0) * SIGMA
    high = table.astype(ml_dtypes.bfloat16)
    low = (table - high.astype(np.float64)).astype(ml_dtypes.bfloat16)
    return np.concatenate([high, low], axis=0)


def lane_sums(x):
    acc = x[:, 0:128]
    for t in range(1, x.shape[1] // 128):
        acc = acc + x[:, t * 128 : (t + 1) * 128]
    return jnp.sum(acc, axis=0, keepdims=True)


def nt_dot(a, b):
    return lax.dot_general(a, b, (((1,), (1,)), ((), ())), preferred_element_type=F32)


def kernel(
    table_ref, traces_ref, oper_ref, out_ref,
    tb, tr, op, s32, f32s, sb, rb, xu, xy, ps, pr, cc, cs, cr, cl, clr, vop, xc, eye, ot, yy, zz, tmp,
    ar_src, ar1, ar_mid, ar2,
    tb_sem, tr_sem, op_sem, a_ss, a_rs, p_ss, p_rs, x_ss, x_rs, g_ss, g_rs, l_ss, l_rs, r_ss, r_rs,
):
    f = lax.axis_index("freq")
    r = lax.axis_index("rcv")
    h = r // 2
    e = lax.rem(r, 2)
    sib = (f, h * 2 + 1 - e)
    xp = (f, (1 - h) * 2 + e)
    g1 = lax.rem(f, 16)
    fy = f // 16
    fz = g1 // 2
    fl = lax.rem(f, 2)

    def peer1(d):
        return (fy * 16 + lax.rem(g1 + d, 16), r)

    def peer2(d):
        return (lax.rem(fy + d // 4, 4) * 16 + g1, lax.rem(r + lax.rem(d, 4), 4))

    def local(src, dst, sem):
        return pltpu.make_async_copy(src, dst, sem)

    def remote(src, dst, ss, rs, to):
        return pltpu.make_async_remote_copy(
            src_ref=src, dst_ref=dst, send_sem=ss, recv_sem=rs, device_id=to, device_id_type=MESH
        )

    flying = {}

    def launch(key, copy):
        copy.start()
        flying[key, "send"] = copy.wait_send
        flying[key, "recv"] = copy.wait_recv

    def land(*key):
        flying.pop((key, "recv"))()

    tb_copy = local(table_ref, tb, tb_sem)
    tb_copy.start()
    flying[("tb",), "recv"] = tb_copy.wait
    tr_copies = [local(traces_ref.at[s], tr.at[s], tr_sem.at[s]) for s in range(2)]
    for s in range(2):
        tr_copies[s].start()
        flying[("tr", s), "recv"] = tr_copies[s].wait

    barrier = pltpu.get_barrier_semaphore()

    def each_freq_peer(act):
        for dz in FAR_FIRST:

            def go(q, c, dz=dz):
                y = lax.rem(fy + q // 2, 4)
                z = lax.rem(fz + dz, 8)
                lo = lax.rem(fl + lax.rem(q, 2), 2)
                act(y * 16 + z * 2 + lo)
                return c

            lax.fori_loop(1 if dz == 0 else 0, 8, go, 0)

    def greet2(d, c):
        to = (lax.rem(fy + d // 3, 4) * 16 + g1, lax.rem(r + 1 + lax.rem(d, 3), 4))
        pl.semaphore_signal(barrier, inc=1, device_id=to, device_id_type=MESH)
        return c

    def greet(to):
        pl.semaphore_signal(barrier, inc=1, device_id=(to, r), device_id_type=MESH)

    lax.fori_loop(0, 12, greet2, 0)
    each_freq_peer(greet)

    op_copy = local(oper_ref, op, op_sem)
    op_copy.start()
    flying[("op",), "recv"] = op_copy.wait

    def dft(s):
        land("tr", s)
        for q in range(4):
            res = nt_dot(tb[...], tr[s, q * 256 : (q + 1) * 256, :])
            d = res[0:128] + res[128:256]
            for c in range(2):
                for qq in range(2):
                    s32[pl.ds((q * 2 + qq) * 2 + c, FREQS, stride=16), :] = d[
                        c * 64 : (c + 1) * 64, qq * 128 : (qq + 1) * 128
                    ]
        sb[:, s * 16 : (s + 1) * 16, :] = s32[...].astype(BF16).reshape(FREQS, 16, 128)

    def a2a_send(s):
        def go(to):
            part = pl.ds(s * 16, 16)
            remote(sb.at[to, part], rb.at[f, part], a_ss.at[s], a_rs.at[s], (to, r)).start()

        each_freq_peer(go)
        rb[f, s * 16 : (s + 1) * 16] = sb[f, s * 16 : (s + 1) * 16]
        most = (pl.ds(0, FREQS - 1), pl.ds(s * 16, 16))
        sent, got = sb.at[most], rb.at[most]
        flying[("a2a", s), "send"] = local(sent, sent, a_ss.at[s]).wait
        flying[("a2a", s), "recv"] = local(got, got, a_rs.at[s]).wait

    def relayout(s):
        f32s[...] = rb[:, s * 16 : (s + 1) * 16, :].astype(F32).reshape(FREQS * 16, 128)
        total = jnp.zeros((FREQS, 128), F32)
        for q in range(8):
            lo, hi = q * 128, (q + 1) * 128
            re = f32s[pl.ds(q * 2, FREQS, stride=16), :]
            im = f32s[pl.ds(q * 2 + 1, FREQS, stride=16), :]
            total = total + re * re + im * im
            reb, imb = re.astype(BF16), im.astype(BF16)
            xu[s, 0:64, lo:hi] = reb
            xu[s, 64:128, lo:hi] = imb
            xu[s, 0:64, ROWS + lo : ROWS + hi] = imb
            xu[s, 64:128, ROWS + lo : ROWS + hi] = -reb
        return jnp.sum(total, axis=0, keepdims=True)

    def cols(b):
        return pl.ds(pl.multiple_of(b * BLK, BLK), BLK)

    def sib_copy(k, s, i):
        return remote(ps.at[k, s, i], pr.at[k, s, i], p_ss.at[k, s, i], p_rs.at[k, s, i], sib)

    def x_copy(k, s, i):
        return remote(cs.at[k, s, i], cr.at[k, s, i], x_ss.at[k, s, i], x_rs.at[k, s, i], xp)

    def ag_copy(k, s, i, b):
        part = vop.at[k, s, b]
        return remote(part, part, g_ss.at[k, s, i], g_rs.at[k, s, i], sib)

    def lo_copy(s):
        return remote(cl.at[s, 1 - h], clr.at[s], l_ss.at[s], l_rs.at[s], xp)

    def adjoint(k, x, s):
        for i in range(2):
            ps[k, s, i] = jnp.dot(x[s], op[:, cols(2 * i + 1 - e)], preferred_element_type=F32)
            launch(("sib", k, s, i), sib_copy(k, s, i))
        for i in range(2):
            p = jnp.dot(x[s], op[:, cols(2 * i + e)], preferred_element_type=F32)
            land("sib", k, s, i)
            c = p + pr[k, s, i]
            cb = c.astype(BF16)
            cc[k, s, i] = c
            cs[k, s, i] = cb
            if k == 0:
                cl[s, i] = (c - cb.astype(F32)).astype(BF16)
            launch(("x", k, s, i), x_copy(k, s, i))

    def gather(k, s, i):
        land("x", k, s, i)
        v = cc[k, s, i] + cr[k, s, i].astype(F32)
        cc[k, s, i] = v
        vop[k, s, 2 * i + e] = v.astype(BF16)
        launch(("ag", k, s, i), ag_copy(k, s, i, 2 * i + e))

    def transpose_operator():
        at = [lax.broadcasted_iota(jnp.int32, (256, 256), d) for d in range(2)]
        eye[...] = jnp.where(at[0] == at[1], 1.0, 0.0).astype(BF16)

        def go(b, c):
            for q in range(2):
                for part in range(2):
                    for n in range(2):
                        rows = slice(part * ROWS + n * 512, part * ROWS + (n + 1) * 512)
                        col = pl.multiple_of(b * BLK + q * 256, 256)
                        ot[b, part * BLK + q * 256 : part * BLK + (q + 1) * 256, n * 512 : (n + 1) * 512] = nt_dot(
                            eye[...], op[rows, pl.ds(col, 256)]
                        ).astype(BF16)
            return c

        lax.fori_loop(0, 4, go, 0)

    def forward_block(k, s, b, dst, first):
        v = vop[k, s, b]
        xc[:, 0:BLK] = v
        xc[0:64, BLK:] = -v[64:128]
        xc[64:128, BLK:] = v[0:64]
        for n in range(2):
            lo, hi = n * 512, (n + 1) * 512
            part = jnp.dot(xc[...], ot[b, :, lo:hi], preferred_element_type=F32)
            if first:
                dst[s, :, lo:hi] = part
            else:
                dst[s, :, lo:hi] += part

    def forward(k, s, i, dst):
        forward_block(k, s, 2 * i + e, dst, i == 0)
        land("ag", k, s, i)
        forward_block(k, s, 2 * i + 1 - e, dst, False)

    def operand(s):
        y = (yy[s] * TAU).astype(BF16)
        xy[s, :, 0:ROWS] = y
        xy[s, 0:64, ROWS:] = y[64:128]
        xy[s, 64:128, ROWS:] = -y[0:64]

    def ar_start(n, tile):
        ar_src[n] = tile
        ar1[n, 0] = tile

        for d in AR_NEAR:
            remote(ar_src.at[n], ar1.at[n, d], r_ss.at[n, 0], r_rs.at[n, 0], peer1(d)).start()
        ar_flying(n, 0, ar1)

    def ar_flying(n, stage, ref):
        part = ref.at[n, pl.ds(1, 15)]
        flying[("ar", n, stage), "send"] = local(part, part, r_ss.at[n, stage]).wait
        flying[("ar", n, stage), "recv"] = local(part, part, r_rs.at[n, stage]).wait

    def ar_middle(n):
        land("ar", n, 0)
        tile = jnp.sum(ar1[n], axis=0)
        ar_mid[n] = tile
        ar2[n, 0] = tile

        for d in AR_FAR:
            remote(ar_mid.at[n], ar2.at[n, d], r_ss.at[n, 1], r_rs.at[n, 1], peer2(d)).start()
        ar_flying(n, 1, ar2)

    def ar_end(n):
        land("ar", n, 1)
        return jnp.sum(jnp.sum(ar2[n], axis=0), axis=1, keepdims=True)

    def tile_of(rows):
        at = lax.broadcasted_iota(jnp.int32, (8, 128), 0)
        tile = jnp.zeros((8, 128), F32)
        for i, row in enumerate(rows):
            tile = jnp.where(at == i, row, tile)
        return tile

    def body():
        land("tb")
        dft(0)
        dft(1)
        pl.semaphore_wait(barrier, FREQS - 1 + 12)
        a2a_send(0)
        a2a_send(1)
        land("op")
        transpose_operator()

        zero = jnp.zeros((1, 128), F32)
        sum_u = zero
        for s in range(2):
            land("a2a", s)
            sum_u = sum_u + relayout(s)
            adjoint(0, xu, s)

        sum_v, sum_y, sum_yu = zero, zero, zero
        for s in range(2):
            for i in range(2):
                gather(0, s, i)
                forward(0, s, i, yy)
            if s == 0:
                operand(s)
                adjoint(1, xy, s)
            v = cc[0, s, h]
            sum_v = sum_v + lane_sums(v * v)
            sum_y = sum_y + lane_sums(yy[s] * yy[s])
            sum_yu = sum_yu + lane_sums(yy[s] * xu[s, :, 0:ROWS].astype(F32))
        ar_start(0, tile_of([sum_u, sum_v, sum_y, sum_yu]))
        operand(1)
        adjoint(1, xy, 1)

        gather(1, 0, 0)
        forward(1, 0, 0, zz)
        ar_middle(0)
        gather(1, 0, 1)
        forward(1, 0, 1, zz)

        total = ar_end(0)
        s_u, s_v, s_y, s_yu = (total[i : i + 1] for i in range(4))
        beta0 = jnp.sqrt(s_u * (1.0 / SIGMA**2) + EPS)
        sb0 = beta0 * SIGMA
        alpha0_sq = s_v / (sb0 * sb0) + EPS
        alpha0 = jnp.sqrt(alpha0_sq)
        g0 = sb0 * alpha0
        s_left = jnp.maximum(s_y - alpha0_sq * (2.0 * s_yu - alpha0_sq * s_u), 0.0)
        beta1_sq = s_left / (g0 * g0) + EPS
        beta1 = jnp.sqrt(beta1_sq)
        k1 = (alpha0_sq + beta1_sq) * TAU

        sum_r, sum_g, sum_gl = zero, zero, zero
        for s in range(2):
            if s == 1:
                gather(1, 1, 0)
                forward(1, 1, 0, zz)
                gather(1, 1, 1)
                for t in range(2):
                    launch(("lo", t), lo_copy(t))
                forward(1, 1, 1, zz)
            right = cc[1, s, h] - k1 * cc[0, s, h]
            sum_r = sum_r + lane_sums(right * right)
            y = yy[s]
            left = y - alpha0_sq * xu[s, :, 0:ROWS].astype(F32)
            ahead = zz[s] - k1 * y
            sum_g = sum_g + lane_sums(ahead * ahead)
            sum_gl = sum_gl + lane_sums(ahead * left)
        ar_start(1, tile_of([sum_r, sum_g, sum_gl]))
        for s in range(2):
            land("lo", s)
        ar_middle(1)
        total = ar_end(1)
        s_r, s_g, s_gl = (total[i : i + 1] for i in range(3))
        g1s = g0 * beta1 * TAU
        alpha1_sq = s_r / (g1s * g1s) + EPS
        alpha1 = jnp.sqrt(alpha1_sq)
        g2s = g1s * alpha1
        a_sq = alpha1_sq * TAU
        s_left2 = jnp.maximum(s_g - a_sq * (2.0 * s_gl - a_sq * s_left), 0.0)
        beta2_sq = s_left2 / (g2s * g2s) + EPS

        rho1_sq = alpha0_sq + beta1_sq
        rho1 = jnp.sqrt(rho1_sq)
        cos1 = alpha0 / rho1
        sin1 = beta1 / rho1
        theta1 = sin1 * alpha1
        rhobar = cos1 * alpha1
        phi1 = cos1 * beta0
        phibar = sin1 * beta0
        rho2 = jnp.sqrt(rhobar * rhobar + beta2_sq)
        phi2 = (rhobar / rho2) * phibar
        y2 = -(phi2 / rho2)
        c_v = (phi1 / rho1 - y2 * (theta1 / rho1)) / g0
        c_r = y2 / g2s
        for s in range(2):
            v = cc[0, s, h] + clr[s].astype(F32)
            right = cc[1, s, h] - k1 * v
            x = c_v * v + c_r * right
            for c in range(2):
                for t in range(4):
                    tmp[t, pl.ds(c * 128 + s, 64, stride=2), :] = x[
                        c * 64 : (c + 1) * 64, t * 128 : (t + 1) * 128
                    ]
        for c in range(2):
            for t in range(4):
                out_ref[pl.ds(t * 256 + c, 128, stride=2), :] = tmp[t, c * 128 : (c + 1) * 128, :].T

    body()
    for wait in flying.values():
        wait()


def per_device(table, traces, downgoing):
    vmem = pltpu.VMEM
    dma = pltpu.SemaphoreType.DMA
    scratch = [
        vmem((4 * FREQS, SAMPLES), BF16),
        vmem((2, ROWS, SAMPLES), BF16),
        vmem((2 * ROWS, COLS), BF16),
        vmem((FREQS * 16, 128), F32),
        vmem((FREQS * 16, 128), F32),
        vmem((FREQS, 32, 128), BF16),
        vmem((FREQS, 32, 128), BF16),
        vmem((2, M, 2 * ROWS), BF16),
        vmem((2, M, 2 * ROWS), BF16),
        vmem((2, 2, 2, M, BLK), F32),
        vmem((2, 2, 2, M, BLK), F32),
        vmem((2, 2, 2, M, BLK), F32),
        vmem((2, 2, 2, M, BLK), BF16),
        vmem((2, 2, 2, M, BLK), BF16),
        vmem((2, 2, M, BLK), BF16),
        vmem((2, M, BLK), BF16),
        vmem((2, 2, 4, M, BLK), BF16),
        vmem((M, 2 * BLK), BF16),
        vmem((256, 256), BF16),
        vmem((4, 2 * BLK, ROWS), BF16),
        vmem((2, M, ROWS), F32),
        vmem((2, M, ROWS), F32),
        vmem((4, 2 * M, 128), F32),
        vmem((2, 8, 128), F32),
        vmem((2, 16, 8, 128), F32),
        vmem((2, 8, 128), F32),
        vmem((2, 16, 8, 128), F32),
        dma, dma((2,)), dma,
        dma((2,)), dma((2,)),
        dma((2, 2, 2)), dma((2, 2, 2)),
        dma((2, 2, 2)), dma((2, 2, 2)),
        dma((2, 2, 2)), dma((2, 2, 2)),
        dma((2,)), dma((2,)),
        dma((2, 2)), dma((2, 2)),
    ]
    out = pl.pallas_call(
        kernel,
        out_shape=jax.ShapeDtypeStruct((2 * BLK, 128), F32),
        in_specs=[
            pl.BlockSpec(memory_space=pl.ANY),
            pl.BlockSpec(memory_space=pl.ANY),
            pl.BlockSpec(memory_space=pl.ANY),
        ],
        out_specs=pl.BlockSpec(memory_space=pltpu.VMEM),
        scratch_shapes=scratch,
        compiler_params=pltpu.CompilerParams(
            collective_id=0, has_side_effects=True, vmem_limit_bytes=63 * 2**20
        ),
        name="lsqr",
    )(table, traces, downgoing.reshape(2 * ROWS, COLS))
    return out.reshape(1, BLK, 2, 128)


def solution(mesh):
    table = dft_table()
    return jax.shard_map(
        lambda traces, downgoing: per_device(jnp.asarray(table), traces, downgoing),
        mesh=mesh,
        in_specs=(P("freq", "rcv", None), P("freq", None, "rcv", None)),
        out_specs=P("freq", "rcv", None, None),
        check_vma=False,
    )
```

time: 91.2 us -> 72.3 us (0.79)
  Pallas kernels: 89.2 us -> 70.3 us
    pallas_call x1, Pallas kernels: 89.2 us -> 70.3 us  [per_device(): pl.pallas_call(kernel, out_shape=jax.ShapeDtypeStruct((2 * BLK, 128), F32...]
    unnamed x3 -> x1, local copies, waits for them, and re-layouts: 1.84 us -> 1.87 us
where the time goes in v2:
time: 72.3 us; the launch traced here: 72.2 us
  Pallas kernels  70.3 us (97%)
  local copies, waits for them, and re-layouts  1.87 us (3%)
    pallas_call x1, Pallas kernels, per_device(): pl.pallas_call(kernel, out_shape=jax.ShapeDtypeStruct((2 * BLK, 128), F32...  70.3 us
    unnamed x1, local copies, waits for them, and re-layouts  1.87 us

profile of v2, /device:TPU:1, one launch (start us, length us, event | category | flops | bytes accessed | tf_op | source)
XLA Modules:
  0.0 72.2 jit_solution(13080602048338104228)
XLA Ops:
  0.0 70.3 %lsqr.1 = f32[1024,128]{1,0:T(8,128)} custom-call(bf16[256,1024]{1,0:T(8,128)(2,1)} %constant.2.clone.table_ref, bf16[2,1024,1024]{2,1,0:T(8,128)(2,1)} %traces_ref.1, bf16[2048,2048]{1,0:T(8,128)(2,1)} %bitcast.2), custom_call_target="tpu_custom_call" | custom-call | tf_op jit(solution)/shard_map/lsqr/pallas_call | solution.py:432
  70.3 1.9 %copy.5 = f32[1,512,2,128]{3,2,1,0:T(2,128)} copy(f32[1,512,2,128]{3,2,1,0:T(2,128)} %bitcast.3) | data formatting | bytes 1048576

commit v3 on v2

--- a/solution.py
+++ b/solution.py
@@ -281,12 +281,12 @@
     def body():
         land("tb")
         dft(0)
-        dft(1)
         pl.semaphore_wait(barrier, FREQS - 1 + 12)
         a2a_send(0)
-        a2a_send(1)
+        dft(1)
         land("op")
         transpose_operator()
+        a2a_send(1)
 
         zero = jnp.zeros((1, 128), F32)
         sum_u = zero
@@ -300,25 +300,46 @@
             for i in range(2):
                 gather(0, s, i)
                 forward(0, s, i, yy)
-            if s == 0:
-                operand(s)
-                adjoint(1, xy, s)
+            operand(s)
+            adjoint(1, xy, s)
             v = cc[0, s, h]
             sum_v = sum_v + lane_sums(v * v)
             sum_y = sum_y + lane_sums(yy[s] * yy[s])
             sum_yu = sum_yu + lane_sums(yy[s] * xu[s, :, 0:ROWS].astype(F32))
-        ar_start(0, tile_of([sum_u, sum_v, sum_y, sum_yu]))
-        operand(1)
-        adjoint(1, xy, 1)
-
-        gather(1, 0, 0)
-        forward(1, 0, 0, zz)
+            if s == 0:
+                ar_start(0, tile_of([sum_u, sum_v, sum_y]))
         ar_middle(0)
-        gather(1, 0, 1)
-        forward(1, 0, 1, zz)
-
+
+        sum_r, sum_rv, sum_g, sum_gy, sum_gu = zero, zero, zero, zero, zero
+        for i in range(2):
+            gather(1, 0, i)
+            forward(1, 0, i, zz)
+        gather(1, 1, 0)
+        forward(1, 1, 0, zz)
         total = ar_end(0)
-        s_u, s_v, s_y, s_yu = (total[i : i + 1] for i in range(4))
+        s_u = total[0:1]
+        kappa = total[2:3] / jnp.maximum(total[1:2], 1e-30) * TAU
+        for s in range(2):
+            if s == 1:
+                gather(1, 1, 1)
+                for t in range(2):
+                    launch(("lo", t), lo_copy(t))
+                forward(1, 1, 1, zz)
+            v = cc[0, s, h]
+            right = cc[1, s, h] - kappa * v
+            sum_r = sum_r + lane_sums(right * right)
+            sum_rv = sum_rv + lane_sums(right * v)
+            y = yy[s]
+            ahead = zz[s] - kappa * y
+            sum_g = sum_g + lane_sums(ahead * ahead)
+            sum_gy = sum_gy + lane_sums(ahead * y)
+            sum_gu = sum_gu + lane_sums(ahead * xu[s, :, 0:ROWS].astype(F32))
+        ar_start(1, tile_of([sum_v, sum_y, sum_yu, sum_r, sum_rv, sum_g, sum_gy, sum_gu]))
+        for s in range(2):
+            land("lo", s)
+        ar_middle(1)
+        total = ar_end(1)
+        s_v, s_y, s_yu, s_r, s_rv, s_g, s_gy, s_gu = (total[i : i + 1] for i in range(8))
         beta0 = jnp.sqrt(s_u * (1.0 / SIGMA**2) + EPS)
         sb0 = beta0 * SIGMA
         alpha0_sq = s_v / (sb0 * sb0) + EPS
@@ -328,29 +349,10 @@
         beta1_sq = s_left / (g0 * g0) + EPS
         beta1 = jnp.sqrt(beta1_sq)
         k1 = (alpha0_sq + beta1_sq) * TAU
-
-        sum_r, sum_g, sum_gl = zero, zero, zero
-        for s in range(2):
-            if s == 1:
-                gather(1, 1, 0)
-                forward(1, 1, 0, zz)
-                gather(1, 1, 1)
-                for t in range(2):
-                    launch(("lo", t), lo_copy(t))
-                forward(1, 1, 1, zz)
-            right = cc[1, s, h] - k1 * cc[0, s, h]
-            sum_r = sum_r + lane_sums(right * right)
-            y = yy[s]
-            left = y - alpha0_sq * xu[s, :, 0:ROWS].astype(F32)
-            ahead = zz[s] - k1 * y
-            sum_g = sum_g + lane_sums(ahead * ahead)
-            sum_gl = sum_gl + lane_sums(ahead * left)
-        ar_start(1, tile_of([sum_r, sum_g, sum_gl]))
-        for s in range(2):
-            land("lo", s)
-        ar_middle(1)
-        total = ar_end(1)
-        s_r, s_g, s_gl = (total[i : i + 1] for i in range(3))
+        delta = k1 - kappa
+        s_r = jnp.maximum(s_r - delta * (2.0 * s_rv - delta * s_v), 0.0)
+        s_gl = s_gy - alpha0_sq * s_gu - delta * (s_y - alpha0_sq * s_yu)
+        s_g = jnp.maximum(s_g - delta * (2.0 * s_gy - delta * s_y), 0.0)
         g1s = g0 * beta1 * TAU
         alpha1_sq = s_r / (g1s * g1s) + EPS
         alpha1 = jnp.sqrt(alpha1_sq)

time: 72.3 us -> 70 us (0.968)
  Pallas kernels: 70.3 us -> 68 us
    pallas_call x1, Pallas kernels: 70.3 us -> 68 us  [per_device(): pl.pallas_call(kernel, out_shape=jax.ShapeDtypeStruct((2 * BLK, 128), F32...]
where the time goes in v3:
time: 70 us; the launch traced here: 69.9 us
  Pallas kernels  68 us (97%)
  local copies, waits for them, and re-layouts  1.87 us (3%)
    pallas_call x1, Pallas kernels, per_device(): pl.pallas_call(kernel, out_shape=jax.ShapeDtypeStruct((2 * BLK, 128), F32...  68 us
    unnamed x1, local copies, waits for them, and re-layouts  1.87 us

profile of v3, /device:TPU:1, one launch (start us, length us, event | category | flops | bytes accessed | tf_op | source)
XLA Modules:
  0.0 69.9 jit_solution(6752261148308524909)
XLA Ops:
  0.0 68.0 %lsqr.1 = f32[1024,128]{1,0:T(8,128)} custom-call(bf16[256,1024]{1,0:T(8,128)(2,1)} %constant.2.clone.table_ref, bf16[2,1024,1024]{2,1,0:T(8,128)(2,1)} %traces_ref.1, bf16[2048,2048]{1,0:T(8,128)(2,1)} %bitcast.2), custom_call_target="tpu_custom_call" | custom-call | tf_op jit(solution)/shard_map/lsqr/pallas_call | solution.py:434
  68.0 1.9 %copy.5 = f32[1,512,2,128]{3,2,1,0:T(2,128)} copy(f32[1,512,2,128]{3,2,1,0:T(2,128)} %bitcast.3) | data formatting | bytes 1048576

commit v4 on v3

--- a/solution.py
+++ b/solution.py
@@ -182,13 +182,19 @@
         return remote(cl.at[s, 1 - h], clr.at[s], l_ss.at[s], l_rs.at[s], xp)
 
     def adjoint(k, x, s):
+        def part(b):
+            return jnp.dot(x[s], op[:, cols(b)], preferred_element_type=F32)
+
+        ps[k, s, 0] = part(1 - e)
+        launch(("sib", k, s, 0), sib_copy(k, s, 0))
+        cc[k, s, 0] = part(e)
+        ps[k, s, 1] = part(2 + 1 - e)
+        launch(("sib", k, s, 1), sib_copy(k, s, 1))
         for i in range(2):
-            ps[k, s, i] = jnp.dot(x[s], op[:, cols(2 * i + 1 - e)], preferred_element_type=F32)
-            launch(("sib", k, s, i), sib_copy(k, s, i))
-        for i in range(2):
-            p = jnp.dot(x[s], op[:, cols(2 * i + e)], preferred_element_type=F32)
+            if i == 1:
+                cc[k, s, 1] = part(2 + e)
             land("sib", k, s, i)
-            c = p + pr[k, s, i]
+            c = cc[k, s, i] + pr[k, s, i]
             cb = c.astype(BF16)
             cc[k, s, i] = c
             cs[k, s, i] = cb
@@ -320,23 +326,23 @@
         s_u = total[0:1]
         kappa = total[2:3] / jnp.maximum(total[1:2], 1e-30) * TAU
         for s in range(2):
+            zz[s] -= kappa * yy[s]
             if s == 1:
                 gather(1, 1, 1)
                 for t in range(2):
                     launch(("lo", t), lo_copy(t))
-                forward(1, 1, 1, zz)
             v = cc[0, s, h]
             right = cc[1, s, h] - kappa * v
             sum_r = sum_r + lane_sums(right * right)
             sum_rv = sum_rv + lane_sums(right * v)
+            if s == 1:
+                forward(1, 1, 1, zz)
             y = yy[s]
-            ahead = zz[s] - kappa * y
+            ahead = zz[s]
             sum_g = sum_g + lane_sums(ahead * ahead)
             sum_gy = sum_gy + lane_sums(ahead * y)
             sum_gu = sum_gu + lane_sums(ahead * xu[s, :, 0:ROWS].astype(F32))
         ar_start(1, tile_of([sum_v, sum_y, sum_yu, sum_r, sum_rv, sum_g, sum_gy, sum_gu]))
-        for s in range(2):
-            land("lo", s)
         ar_middle(1)
         total = ar_end(1)
         s_v, s_y, s_yu, s_r, s_rv, s_g, s_gy, s_gu = (total[i : i + 1] for i in range(8))
@@ -375,6 +381,7 @@
         c_v = (phi1 / rho1 - y2 * (theta1 / rho1)) / g0
         c_r = y2 / g2s
         for s in range(2):
+            land("lo", s)
             v = cc[0, s, h] + clr[s].astype(F32)
             right = cc[1, s, h] - k1 * v
             x = c_v * v + c_r * right

time: 70 us -> 69.3 us (0.990)
  Pallas kernels: 68 us -> 67.3 us
    pallas_call x1, Pallas kernels: 68 us -> 67.3 us  [per_device(): pl.pallas_call(kernel, out_shape=jax.ShapeDtypeStruct((2 * BLK, 128), F32...]
where the time goes in v4:
time: 69.3 us; the launch traced here: 69.1 us
  Pallas kernels  67.3 us (97%)
  local copies, waits for them, and re-layouts  1.87 us (3%)
    pallas_call x1, Pallas kernels, per_device(): pl.pallas_call(kernel, out_shape=jax.ShapeDtypeStruct((2 * BLK, 128), F32...  67.3 us
    unnamed x1, local copies, waits for them, and re-layouts  1.87 us

profile of v4, /device:TPU:1, one launch (start us, length us, event | category | flops | bytes accessed | tf_op | source)
XLA Modules:
  0.0 69.1 jit_solution(18358699696931099783)
XLA Ops:
  0.0 67.3 %lsqr.1 = f32[1024,128]{1,0:T(8,128)} custom-call(bf16[256,1024]{1,0:T(8,128)(2,1)} %constant.2.clone.table_ref, bf16[2,1024,1024]{2,1,0:T(8,128)(2,1)} %traces_ref.1, bf16[2048,2048]{1,0:T(8,128)(2,1)} %bitcast.2), custom_call_target="tpu_custom_call" | custom-call | tf_op jit(solution)/shard_map/lsqr/pallas_call | solution.py:441
  67.3 1.9 %copy.5 = f32[1,512,2,128]{3,2,1,0:T(2,128)} copy(f32[1,512,2,128]{3,2,1,0:T(2,128)} %bitcast.3) | data formatting | bytes 1048576

commit v5 on v4

--- a/solution.py
+++ b/solution.py
@@ -103,13 +103,17 @@
         for dz in FAR_FIRST:
 
             def go(q, c, dz=dz):
-                y = lax.rem(fy + q // 2, 4)
+                y = lax.rem(fy + 2 + q // 2, 4)
                 z = lax.rem(fz + dz, 8)
-                lo = lax.rem(fl + lax.rem(q, 2), 2)
+                lo = lax.rem(fl + 1 + lax.rem(q, 2), 2)
                 act(y * 16 + z * 2 + lo)
                 return c
 
-            lax.fori_loop(1 if dz == 0 else 0, 8, go, 0)
+            if dz == 0:
+                lax.fori_loop(0, 5, go, 0)
+                lax.fori_loop(6, 8, go, 0)
+            else:
+                lax.fori_loop(0, 8, go, 0)
 
     def greet2(d, c):
         to = (lax.rem(fy + d // 3, 4) * 16 + g1, lax.rem(r + 1 + lax.rem(d, 3), 4))
@@ -196,18 +200,18 @@
             land("sib", k, s, i)
             c = cc[k, s, i] + pr[k, s, i]
             cb = c.astype(BF16)
+            cs[k, s, i] = cb
+            launch(("x", k, s, i), x_copy(k, s, i))
             cc[k, s, i] = c
-            cs[k, s, i] = cb
             if k == 0:
                 cl[s, i] = (c - cb.astype(F32)).astype(BF16)
-            launch(("x", k, s, i), x_copy(k, s, i))
 
     def gather(k, s, i):
         land("x", k, s, i)
         v = cc[k, s, i] + cr[k, s, i].astype(F32)
-        cc[k, s, i] = v
         vop[k, s, 2 * i + e] = v.astype(BF16)
         launch(("ag", k, s, i), ag_copy(k, s, i, 2 * i + e))
+        cc[k, s, i] = v
 
     def transpose_operator():
         at = [lax.broadcasted_iota(jnp.int32, (256, 256), d) for d in range(2)]

time: 69.3 us -> 69 us (level)
  no operation moved by 1% of the time
where the time goes in v5:
time: 69 us; the launch traced here: 68.9 us
  Pallas kernels  67 us (97%)
  local copies, waits for them, and re-layouts  1.87 us (3%)
    pallas_call x1, Pallas kernels, per_device(): pl.pallas_call(kernel, out_shape=jax.ShapeDtypeStruct((2 * BLK, 128), F32...  67 us
    unnamed x1, local copies, waits for them, and re-layouts  1.87 us

profile of v5, /device:TPU:1, one launch (start us, length us, event | category | flops | bytes accessed | tf_op | source)
XLA Modules:
  0.0 68.9 jit_solution(9677614623599556510)
XLA Ops:
  0.0 67.0 %lsqr.1 = f32[1024,128]{1,0:T(8,128)} custom-call(bf16[256,1024]{1,0:T(8,128)(2,1)} %constant.2.clone.table_ref, bf16[2,1024,1024]{2,1,0:T(8,128)(2,1)} %traces_ref.1, bf16[2048,2048]{1,0:T(8,128)(2,1)} %bitcast.2), custom_call_target="tpu_custom_call" | custom-call | tf_op jit(solution)/shard_map/lsqr/pallas_call | solution.py:445
  67.0 1.9 %copy.5 = f32[1,512,2,128]{3,2,1,0:T(2,128)} copy(f32[1,512,2,128]{3,2,1,0:T(2,128)} %bitcast.3) | data formatting | bytes 1048576
